TPU v7x, 512 devices: a whole 4x8x8 slice. The times are simulated.
512 devices in a mesh: sess: 128 (over z, y, core), section: 4 (over x).
Axes of the slice: x: 4, y: 8, z: 8, core: 2. Of those that a mesh axis runs over, the one named last changes fastest.
Arguments:
- new_frames: bfloat16 [4, 1536, 16, 1536], P('section', 'sess'), may hold values from -6 to 6
- conv_edges: bfloat16 [4, 1536, 30, 1536], P('section', 'sess'), may hold values from -5 to 5
- kv_cache: bfloat16 [4, 1536, 64, 1536], P('section', 'sess'), may hold values from -240 to 240, as said below
- norm_gains: float32 [4, 2, 1536], P('section'), may hold values from 0.25 to 1.75
- conv_kernel: float32 [4, 31, 1536], P('section'), may hold values from -1 to 1
- w_qkv: bfloat16 [4, 1536, 2304], P('section', 'sess'), may hold values from -0.15625 to 0.15625
- w_out: bfloat16 [4, 768, 1536], P('section', 'sess'), may hold values from -0.21875 to 0.21875
- move_targets: int32 [1536], P('sess'), may hold values from 0 to 1535, as said below
- lengths: int32 [1536], P('sess'), may hold values from 0 to 64
- counts: int32 [128], P('sess'), may hold values from 6 to 12
Outputs:
- handed: bfloat16 [4, 1536, 16, 1536], P('section', 'sess')
Inputs may be any that keep to these rules, and one draw needn't show every extreme that they name: `move_targets`: each index of sess hands exactly one live session to each of the indices 1 and 2 places away on either side, cyclically, and receives one from each; a session leaving for the index o places ahead is replaced by the one arriving from o places behind. All other sessions stay in their slots. `kv_cache`: values are of order one; keys may be up to 240 in magnitude.
All inputs are finite; a program needn't handle non-finite values.
Results may differ from a plain program's by a relative error of at most 0.0093.
The roundings to bfloat16 on the way count: a program that leaves them out, or rounds other values in their place, can miss the bound.
Values may be sent and summed in bfloat16 or wider, within the bound.
A program may use at most 128 MiB of HBM per device.

v0:
```python
import jax
import jax.numpy as jnp
from jax import lax
from jax.sharding import PartitionSpec as P

D = 1536
HEADS = 8
HSIZE = 96
HD = 768
KERNEL = 31
CTX = 64
FR = 16


OFFSETS = (1, -1, 2, -2)


def passed_along(x, axis, by):
    size = lax.axis_size(axis)
    return lax.ppermute(x, axis, [(i, (i + by) % size) for i in range(size)])


def layer_norm(values, gain):
    center = values - jnp.mean(values, axis=-1, keepdims=True)
    spread = jnp.mean(center * center, axis=-1, keepdims=True)
    return center * lax.rsqrt(spread + 1e-05) * gain


def attend(queries, keys, values, ctx_lengths):
    session_count = queries.shape[0]
    query_heads = queries.reshape(session_count, FR, HEADS, HSIZE)
    key_heads = keys.reshape(session_count, CTX + FR, HEADS, HSIZE)
    value_heads = values.reshape(session_count, CTX + FR, HEADS, HSIZE)
    scores = jnp.einsum(
        "sthd,suhd->shtu", query_heads, key_heads, preferred_element_type=jnp.float32
    ) * HSIZE ** (-0.5)
    key_pos = jnp.arange(CTX + FR, dtype=jnp.int32)
    query_pos = jnp.arange(FR, dtype=jnp.int32)
    cached_ok = key_pos[None, :] >= (CTX - ctx_lengths)[:, None]
    fresh_ok = key_pos[None, :] - CTX <= query_pos[:, None]
    allowed = jnp.where(key_pos[None, None, :] < CTX, cached_ok[:, None, :], fresh_ok[None, :, :])
    scores = jnp.where(allowed[:, None, :, :], scores, jnp.float32(-1e30))
    row_max = jnp.max(scores, axis=-1, keepdims=True)
    weights = jnp.exp(scores - row_max)
    probs = (weights / jnp.sum(weights, axis=-1, keepdims=True)).astype(jnp.bfloat16)
    context = jnp.einsum("shtu,suhd->sthd", probs, value_heads, preferred_element_type=jnp.float32)
    return context.astype(jnp.bfloat16).reshape(session_count, FR, HD)


def section_compute(
    frames, conv_edge, cache, ctx_lengths, gains_now, kernel_now, qkv_rows, out_rows
):
    session_count = frames.shape[0]
    normed = layer_norm(frames.astype(jnp.float32), gains_now[0]).astype(jnp.bfloat16)
    sequence = jnp.concatenate([conv_edge, normed], axis=1)
    conv_out = jnp.zeros((session_count, FR, D), jnp.float32)
    for tap in range(KERNEL):
        conv_out = conv_out + kernel_now[tap] * sequence[:, tap : tap + FR].astype(jnp.float32)
    mid_state = frames.astype(jnp.float32) + conv_out
    second = layer_norm(mid_state, gains_now[1]).astype(jnp.bfloat16).reshape(-1, D)
    columns = second
    projected = jnp.dot(
        columns,
        lax.all_gather(qkv_rows, "sess", axis=0, tiled=True),
        preferred_element_type=jnp.float32,
    )
    projected = projected.astype(jnp.bfloat16).reshape(session_count, FR, 3 * HD)
    keys = jnp.concatenate([cache[:, :, :HD], projected[:, :, HD : 2 * HD]], axis=1)
    values = jnp.concatenate([cache[:, :, HD:], projected[:, :, 2 * HD :]], axis=1)
    context = attend(projected[:, :, :HD], keys, values, ctx_lengths).reshape(-1, HD)
    columns = context
    output = jnp.dot(
        columns,
        lax.all_gather(out_rows, "sess", axis=0, tiled=True),
        preferred_element_type=jnp.float32,
    )
    return mid_state + output.reshape(session_count, FR, D)


def body(
    new_frames,
    conv_edges,
    kv_cache,
    norm_gains,
    conv_kernel,
    w_qkv,
    w_out,
    move_targets,
    lengths,
    counts,
):
    slots = new_frames.shape[1]
    width = lax.axis_size("sess")
    my_index = lax.axis_index("sess")
    target_device = move_targets // slots
    picks = []
    for offset in OFFSETS:
        wanted = (my_index + offset) % width
        picks.append(jnp.argmax(target_device == wanted))
    frames_now = new_frames[0]
    edges_now = conv_edges[0]
    cache_now = kv_cache[0]
    gains_now = norm_gains[0]
    kernel_now = conv_kernel[0]
    qkv_rows = w_qkv[0]
    out_rows = w_out[0]
    live_mask = jnp.arange(slots, dtype=jnp.int32) < counts[0]
    moved_edges = edges_now
    moved_cache = cache_now
    for offset, slot_pick in zip(OFFSETS, picks):
        arrived = passed_along((edges_now[slot_pick], cache_now[slot_pick]), "sess", offset)
        moved_edges = moved_edges.at[slot_pick].set(arrived[0])
        moved_cache = moved_cache.at[slot_pick].set(arrived[1])
    result = section_compute(
        frames_now, moved_edges, moved_cache, lengths, gains_now, kernel_now, qkv_rows, out_rows
    ).astype(jnp.bfloat16)
    result = jnp.where(live_mask[:, None, None], result, jnp.zeros_like(result))
    return passed_along(result[None], "section", 1)


def solution(mesh):
    placed = (
        P("section", "sess", None, None),
        P("section", "sess", None, None),
        P("section", "sess", None, None),
        P("section", None, None),
        P("section", None, None),
        P("section", "sess", None),
        P("section", "sess", None),
        P("sess"),
        P("sess"),
        P("sess"),
    )
    return jax.shard_map(
        body,
        mesh=mesh,
        in_specs=placed,
        out_specs=P("section", "sess", None, None),
        check_vma=False,
    )
```

profile of v0, /device:TPU:1, one launch (start us, length us, event | category | flops | bytes accessed | tf_op | source)
XLA Modules:
  0.0 225.7 jit_solution(4468303033332305166)
XLA Ops:
  6.5 1.6 copy.21
  8.3 1.4 compare_reduce_fusion.3
  10.9 1.4 compare_reduce_fusion
  13.5 1.4 compare_reduce_fusion.2
  16.0 1.4 compare_reduce_fusion.1
  21.1 1.1 dynamic-slice_bitcast_fusion.4
  22.3 4.7 %collective-permute-start = (bf16[30,1536]{1,0:T(8,128)(2,1)S(1)}, bf16[30,1536]{1,0:T(8,128)(2,1)}, u32[]{:S(2)}, u32[]{:S(2)}) collective-permute-start(bf16[30,1536]{1,0:T(8,128)(2,1)S(1)} %get-tuple-element.156), channel_id=1, source_target_pairs={{0,4},{4,8},{8,12},{12,16},{16,20},{20,24},{24,28},{28,32},{32,36}... | collective-permute-start | bytes 276488 | tf_op jit(solution)/shard_map/ppermute | solution.py:20
  27.0 6.1 %collective-permute-start.1 = (bf16[30,1536]{1,0:T(8,128)(2,1)S(1)}, bf16[30,1536]{1,0:T(8,128)(2,1)}, u32[]{:S(2)}, u32[]{:S(2)}) collective-permute-start(bf16[30,1536]{1,0:T(8,128)(2,1)S(1)} %get-tuple-element.155), channel_id=1, source_target_pairs={{0,508},{4,0},{8,4},{12,8},{16,12},{20,16},{24,20},{28,24},{32,28}... | collective-permute-start | bytes 276488 | tf_op jit(solution)/shard_map/ppermute | solution.py:20
  33.1 1.9 collective-permute-start.2
  35.1 8.2 %collective-permute-start.3 = (bf16[30,1536]{1,0:T(8,128)(2,1)S(1)}, bf16[30,1536]{1,0:T(8,128)(2,1)S(1)}, u32[]{:S(2)}, u32[]{:S(2)}) collective-permute-start(bf16[30,1536]{1,0:T(8,128)(2,1)S(1)} %get-tuple-element.154), channel_id=1, source_target_pairs={{0,504},{4,508},{8,0},{12,4},{16,8},{20,12},{24,16},{28,20},{32,24... | collective-permute-start | bytes 276488 | tf_op jit(solution)/shard_map/ppermute | solution.py:20
  43.3 1.3 dynamic-slice_bitcast_fusion
  44.6 3.4 %collective-permute-start.4 = (bf16[64,1536]{1,0:T(8,128)(2,1)S(1)}, bf16[64,1536]{1,0:T(8,128)(2,1)S(1)}, u32[]{:S(2)}, u32[]{:S(2)}) collective-permute-start(bf16[64,1536]{1,0:T(8,128)(2,1)S(1)} %get-tuple-element.152), channel_id=1, source_target_pairs={{0,4},{4,8},{8,12},{12,16},{16,20},{20,24},{24,28},{28,32},{32,36}... | collective-permute-start | bytes 589832 | tf_op jit(solution)/shard_map/ppermute | solution.py:20
  48.0 0.6 copy.26
  49.8 1.6 copy-done.1
  51.6 0.5 copy-done.9
  52.8 0.4 fusion.36
  53.2 0.6 broadcast_select_fusion
  53.8 0.8 and_reduce_fusion
  54.7 5.6 %collective-permute-start.5 = (bf16[64,1536]{1,0:T(8,128)(2,1)S(1)}, bf16[64,1536]{1,0:T(8,128)(2,1)S(1)}, u32[]{:S(2)}, u32[]{:S(2)}) collective-permute-start(bf16[64,1536]{1,0:T(8,128)(2,1)S(1)} %get-tuple-element.151), channel_id=1, source_target_pairs={{0,508},{4,0},{8,4},{12,8},{16,12},{20,16},{24,20},{28,24},{32,28}... | collective-permute-start | bytes 589832 | tf_op jit(solution)/shard_map/ppermute | solution.py:20
  60.3 1.6 bitcast_dynamic-update-slice_fusion.1
  61.9 1.9 collective-permute-start.6
  63.8 1.5 fusion.58
  65.3 6.9 %collective-permute-start.7 = (bf16[64,1536]{1,0:T(8,128)(2,1)S(1)}, bf16[64,1536]{1,0:T(8,128)(2,1)S(1)}, u32[]{:S(2)}, u32[]{:S(2)}) collective-permute-start(bf16[64,1536]{1,0:T(8,128)(2,1)S(1)} %get-tuple-element.150), channel_id=1, source_target_pairs={{0,504},{4,508},{8,0},{12,4},{16,8},{20,12},{24,16},{28,20},{32,24... | collective-permute-start | bytes 589832 | tf_op jit(solution)/shard_map/ppermute | solution.py:20
  72.2 0.6 fusion.57
  72.8 0.7 fusion.56
  73.5 7.1 %fusion.60 = (f32[12,16]{1,0:T(8,128)S(1)}, f32[12,16,1536]{2,1,0:T(8,128)S(1)}) fusion(bf16[12,16,1536]{2,1,0:T(8,128)(2,1)S(1)} %fusion.36, f32[1536]{0:T(1024)S(1)} %get-tuple-element.138, bf16[12,30,1536]{2,1,0:T(8,128)(2,1)S(1)} %fusion.56, f32[1536]{0:T(1024)S(1)} %get-tuple-element.139, f32[1536]{0:T(1024)S(1)} %get-tuple-element.110, ...), kind=kLoop, calls=%fused_computation.164 | loop fusion | flops 41287488 | bytes 12641024 | tf_op jit(solution)/shard_map/reduce_sum | solution.py:24
  81.2 0.7 bitcast_dynamic-update-slice_fusion
  81.9 0.6 fusion.55
  82.6 0.6 fusion.54
  83.2 0.7 fusion.53
  83.9 1.7 fusion.62
  85.6 27.0 %all-gather.5.cloned.1.call-done = bf16[1,1536,2304]{2,0,1:T(2,128)(2,1)} async-done(((bf16[1,12,2304]{2,0,1:T(2,128)(2,1)}), bf16[1,1536,2304]{2,0,1:T(2,128)(2,1)}) %all-gather.5.cloned.1.call-update) | async-done | bytes 7077904 | tf_op jit(solution)/shard_map/all_gather | solution.py:64
  112.6 6.7 %fusion.4 = bf16[192,2304]{1,0:T(8,128)(2,1)S(1)} fusion(bf16[192,1536]{1,0:T(8,128)(2,1)S(1)} %bitcast.96, bf16[1,1536,2304]{2,0,1:T(2,128)(2,1)} %all-gather.5.cloned.1.call-done), kind=kOutput, calls=%fused_computation.18 | convolution fusion | flops 1359396864 | bytes 8552448 | tf_op jit(solution)/shard_map/dot_general | solution.py:62
  119.3 0.8 fusion.63
  120.1 0.6 copy-done.2
  120.7 1.4 pad_maximum_fusion
  122.1 3.1 %reshape.438 = bf16[12,80,8,96]{3,2,1,0:T(8,128)(2,1)} reshape(bf16[12,80,768]{2,1,0:T(8,128)(2,1)S(1)} %get-tuple-element.164) | data formatting | bytes 2949120 | tf_op jit(solution)/shard_map/reshape | solution.py:33
  125.2 3.6 %reshape.440 = bf16[12,80,8,96]{3,2,1,0:T(8,128)(2,1)S(1)} reshape(bf16[12,80,768]{2,1,0:T(8,128)(2,1)} %get-tuple-element.163) | data formatting | bytes 2949120 | tf_op jit(solution)/shard_map/reshape | solution.py:32
  128.8 1.4 reshape.439
  130.2 2.8 %fusion.25 = f32[12,8,16,80]{3,2,1,0:T(8,128)} fusion(bf16[12,80,8,96]{3,2,1,0:T(8,128)(2,1)S(1)} %reshape.440, bf16[12,16,8,96]{3,2,1,0:T(8,128)(2,1)S(1)} %reshape.439, pred[12,16,80]{2,1,0:T(8,128)(4,1)} %broadcast_select_fusion), kind=kOutput, calls=%fused_computation.54 | convolution fusion | flops 23838720 | bytes 2276352 | tf_op jit(solution)/shard_map/sthd,suhd->shtu/dot_general | solution.py:34
  132.9 1.9 fusion.64
  134.8 4.8 %fusion.31 = bf16[12,16,8,96]{3,1,2,0:T(8,128)(2,1)S(1)} fusion(bf16[12,80,8,96]{3,2,1,0:T(8,128)(2,1)} %reshape.438, f32[12,8,16]{2,1,0:T(8,128)S(1)} %fusion.64, f32[12,8,16,80]{3,2,1,0:T(8,128)} %fusion.25), kind=kOutput, calls=%fused_computation.56 | convolution fusion | flops 24110672 | bytes 2267136 | tf_op jit(solution)/shard_map/shtu,suhd->sthd/dot_general | solution.py:46
  139.7 0.3 dot_general.17
  140.0 57.2 %all-gather.7.cloned.1.call-done = bf16[1,768,1536]{2,0,1:T(2,128)(2,1)} async-done(((bf16[1,6,1536]{2,0,1:T(2,128)(2,1)}), bf16[1,768,1536]{2,0,1:T(2,128)(2,1)}) %all-gather.7.cloned.1.call-update) | async-done | bytes 2359312 | tf_op jit(solution)/shard_map/all_gather | solution.py:74
  197.3 3.0 %fusion.9 = bf16[1,12,16,1536]{3,2,1,0:T(8,128)(2,1)S(1)} fusion(f32[12,16,1536]{2,1,0:T(8,128)S(1)} %get-tuple-element.147, bf16[12,16,768]{2,1,0:T(8,128)(2,1)S(1)} %dot_general.17, bf16[1,768,1536]{2,0,1:T(2,128)(2,1)} %all-gather.7.cloned.1.call-done, pred[12]{0:T(512)(128)(4,1)S(1)} %iota_compare_fusion.3), kind=kOutput, calls=%fused_computation.36 | convolution fusion | flops 453869568 | bytes 4423692 | tf_op jit(solution)/shard_map/dot_general | solution.py:72
  200.2 3.1 %collective-permute-start.8 = (bf16[1,12,16,1536]{3,2,1,0:T(8,128)(2,1)S(1)}, bf16[1,12,16,1536]{3,2,1,0:T(8,128)(2,1)S(1)}, u32[]{:S(2)}, u32[]{:S(2)}) collective-permute-start(bf16[1,12,16,1536]{3,2,1,0:T(8,128)(2,1)S(1)} %fusion.9), channel_id=1, source_target_pairs={{0,1},{1,2},{2,3},{3,0},{4,5},{5,6},{6,7},{7,4},{8,9},{9,10},{10,1... | collective-permute-start | bytes 1769480 | tf_op jit(solution)/shard_map/ppermute | solution.py:20
  203.3 14.7 %collective-permute-done.8 = bf16[1,12,16,1536]{3,2,1,0:T(8,128)(2,1)S(1)} collective-permute-done((bf16[1,12,16,1536]{3,2,1,0:T(8,128)(2,1)S(1)}, bf16[1,12,16,1536]{3,2,1,0:T(8,128)(2,1)S(1)}, u32[]{:S(2)}, u32[]{:S(2)}) %collective-permute-start.8) | collective-permute-done | bytes 589856 | tf_op jit(solution)/shard_map/ppermute | solution.py:20
  218.0 0.8 copy.63
  (49 shorter events, 2.1 us)
Async XLA Ops:
  6.5 106.1 %all-gather.5.cloned.1.call-start = ((), (), s32[]{:S(2)}) async-start(), calls=%async_computation | async-start | bytes 14266368 | tf_op jit(solution)/shard_map/all_gather | solution.py:64
  8.2 189.1 %all-gather.7.cloned.1.call-start = ((), (), s32[]{:S(2)}) async-start(), calls=%async_computation.1 | async-start | bytes 4755456 | tf_op jit(solution)/shard_map/all_gather | solution.py:74
  21.1 26.9 %copy-start.6 = (bf16[1,6,1536]{2,1,0:T(8,128)(2,1)S(1)}, bf16[1,6,1536]{2,1,0:T(8,128)(2,1)}, u32[]{:S(2)}) copy-start(bf16[1,6,1536]{2,1,0:T(8,128)(2,1)} %param.32) | copy-start | bytes 55300
  21.1 27.5 %copy-start.5 = (f32[1,31,1536]{2,0,1:T(1,128)S(1)}, f32[1,31,1536]{2,0,1:T(1,128)}, u32[]{:S(2)}) copy-start(f32[1,31,1536]{2,0,1:T(1,128)} %param.30) | copy-start | bytes 571396
  22.2 26.9 %copy-start.7 = (f32[1,2,1536]{2,1,0:T(2,128)S(1)}, f32[1,2,1536]{2,1,0:T(2,128)}, u32[]{:S(2)}) copy-start(f32[1,2,1536]{2,1,0:T(2,128)} %param.29) | copy-start | bytes 36868
  22.3 27.0 %copy-start = (bf16[1,12,16,1536]{3,2,1,0:T(8,128)(2,1)S(1)}, bf16[1,12,16,1536]{3,2,1,0:T(8,128)(2,1)}, u32[]{:S(2)}) copy-start(bf16[1,12,16,1536]{3,2,1,0:T(8,128)(2,1)} %param.26) | copy-start | bytes 1769476
  22.3 32.4 %collective-permute-start = (bf16[30,1536]{1,0:T(8,128)(2,1)S(1)}, bf16[30,1536]{1,0:T(8,128)(2,1)}, u32[]{:S(2)}, u32[]{:S(2)}) collective-permute-start(bf16[30,1536]{1,0:T(8,128)(2,1)S(1)} %get-tuple-element.156), channel_id=1, source_target_pairs={{0,4},{4,8},{8,12},{12,16},{16,20},{20,24},{24,28},{28,32},{32,36}... | collective-permute-start | bytes 276488 | tf_op jit(solution)/shard_map/ppermute | solution.py:20
  27.0 34.9 %collective-permute-start.1 = (bf16[30,1536]{1,0:T(8,128)(2,1)S(1)}, bf16[30,1536]{1,0:T(8,128)(2,1)}, u32[]{:S(2)}, u32[]{:S(2)}) collective-permute-start(bf16[30,1536]{1,0:T(8,128)(2,1)S(1)} %get-tuple-element.155), channel_id=1, source_target_pairs={{0,508},{4,0},{8,4},{12,8},{16,12},{20,16},{24,20},{28,24},{32,28}... | collective-permute-start | bytes 276488 | tf_op jit(solution)/shard_map/ppermute | solution.py:20
  33.1 32.2 %collective-permute-start.2 = (bf16[30,1536]{1,0:T(8,128)(2,1)S(1)}, bf16[30,1536]{1,0:T(8,128)(2,1)S(1)}, u32[]{:S(2)}, u32[]{:S(2)}) collective-permute-start(bf16[30,1536]{1,0:T(8,128)(2,1)S(1)} %get-tuple-element.157), channel_id=1, source_target_pairs={{0,8},{4,12},{8,16},{12,20},{16,24},{20,28},{24,32},{28,36},{32,40... | collective-permute-start | bytes 276488 | tf_op jit(solution)/shard_map/ppermute | solution.py:20
  35.1 37.7 %collective-permute-start.3 = (bf16[30,1536]{1,0:T(8,128)(2,1)S(1)}, bf16[30,1536]{1,0:T(8,128)(2,1)S(1)}, u32[]{:S(2)}, u32[]{:S(2)}) collective-permute-start(bf16[30,1536]{1,0:T(8,128)(2,1)S(1)} %get-tuple-element.154), channel_id=1, source_target_pairs={{0,504},{4,508},{8,0},{12,4},{16,8},{20,12},{24,16},{28,20},{32,24... | collective-permute-start | bytes 276488 | tf_op jit(solution)/shard_map/ppermute | solution.py:20
  44.5 5.1 %copy-start.4 = (bf16[1,12,30,1536]{3,2,1,0:T(8,128)(2,1)S(1)}, bf16[1,12,30,1536]{3,2,1,0:T(8,128)(2,1)}, u32[]{:S(2)}) copy-start(bf16[1,12,30,1536]{3,2,1,0:T(8,128)(2,1)} %param.27) | copy-start | bytes 3317764
  44.6 36.6 %collective-permute-start.4 = (bf16[64,1536]{1,0:T(8,128)(2,1)S(1)}, bf16[64,1536]{1,0:T(8,128)(2,1)S(1)}, u32[]{:S(2)}, u32[]{:S(2)}) collective-permute-start(bf16[64,1536]{1,0:T(8,128)(2,1)S(1)} %get-tuple-element.152), channel_id=1, source_target_pairs={{0,4},{4,8},{8,12},{12,16},{16,20},{20,24},{24,28},{28,32},{32,36}... | collective-permute-start | bytes 589832 | tf_op jit(solution)/shard_map/ppermute | solution.py:20
  49.7 1.7 copy-start.1
  51.4 0.7 copy-start.9
  51.6 2.3 %copy-start.8 = (s32[3]{0:T(128)S(1)}, s32[3]{0:T(128)}, u32[]{:S(2)}) copy-start(s32[3]{0:T(128)} %constant.243.clone.1) | copy-start | bytes 40
  54.7 27.3 %collective-permute-start.5 = (bf16[64,1536]{1,0:T(8,128)(2,1)S(1)}, bf16[64,1536]{1,0:T(8,128)(2,1)S(1)}, u32[]{:S(2)}, u32[]{:S(2)}) collective-permute-start(bf16[64,1536]{1,0:T(8,128)(2,1)S(1)} %get-tuple-element.151), channel_id=1, source_target_pairs={{0,508},{4,0},{8,4},{12,8},{16,12},{20,16},{24,20},{28,24},{32,28}... | collective-permute-start | bytes 589832 | tf_op jit(solution)/shard_map/ppermute | solution.py:20
  61.9 20.7 %collective-permute-start.6 = (bf16[64,1536]{1,0:T(8,128)(2,1)S(1)}, bf16[64,1536]{1,0:T(8,128)(2,1)S(1)}, u32[]{:S(2)}, u32[]{:S(2)}) collective-permute-start(bf16[64,1536]{1,0:T(8,128)(2,1)S(1)} %get-tuple-element.153), channel_id=1, source_target_pairs={{0,8},{4,12},{8,16},{12,20},{16,24},{20,28},{24,32},{28,36},{32,40... | collective-permute-start | bytes 589832 | tf_op jit(solution)/shard_map/ppermute | solution.py:20
  65.3 17.9 %collective-permute-start.7 = (bf16[64,1536]{1,0:T(8,128)(2,1)S(1)}, bf16[64,1536]{1,0:T(8,128)(2,1)S(1)}, u32[]{:S(2)}, u32[]{:S(2)}) collective-permute-start(bf16[64,1536]{1,0:T(8,128)(2,1)S(1)} %get-tuple-element.150), channel_id=1, source_target_pairs={{0,504},{4,508},{8,0},{12,4},{16,8},{20,12},{24,16},{28,20},{32,24... | collective-permute-start | bytes 589832 | tf_op jit(solution)/shard_map/ppermute | solution.py:20
  112.6 7.5 %copy-start.3 = (bf16[12,64,768]{2,1,0:T(8,128)(2,1)S(1)}, bf16[12,64,768]{2,1,0:T(8,128)(2,1)}, u32[]{:S(2)}) copy-start(bf16[12,64,768]{2,1,0:T(8,128)(2,1)} %get-tuple-element.149) | copy-start | bytes 3538948
  119.3 1.4 copy-start.2
  200.2 17.8 %collective-permute-start.8 = (bf16[1,12,16,1536]{3,2,1,0:T(8,128)(2,1)S(1)}, bf16[1,12,16,1536]{3,2,1,0:T(8,128)(2,1)S(1)}, u32[]{:S(2)}, u32[]{:S(2)}) collective-permute-start(bf16[1,12,16,1536]{3,2,1,0:T(8,128)(2,1)S(1)} %fusion.9), channel_id=1, source_target_pairs={{0,1},{1,2},{2,3},{3,0},{4,5},{5,6},{6,7},{7,4},{8,9},{9,10},{10,1... | collective-permute-start | bytes 1769480 | tf_op jit(solution)/shard_map/ppermute | solution.py:20
Sparse Core Ops, SparseCore 0:
  10.6 102.0 all-gather.4
  115.8 81.3 all-gather.6
where the time goes:
time: 227 us; the launch traced here: 226 us
  waiting for transfers between devices  99 us (44%)
  starting transfers between devices  41.9 us (18%)
  other arithmetic  25.8 us (11%)
  between operations  21.9 us (10%)
  local copies, waits for them, and re-layouts  20 us (9%)
  matrix products  17.2 us (8%)
    all_gather x1, waiting for transfers between devices, section_compute(): lax.all_gather(out_rows, 'sess', axis=0, tiled=True)  57.2 us
    ppermute x9, starting transfers between devices, passed_along(): return lax.ppermute(x, axis, [(i, (i + by) % size) for i in range(size)])  41.8 us
    all_gather x1, waiting for transfers between devices, section_compute(): lax.all_gather(qkv_rows, 'sess', axis=0, tiled=True)  27 us
    ppermute x9, waiting for transfers between devices, passed_along(): return lax.ppermute(x, axis, [(i, (i + by) % size) for i in range(size)])  14.7 us
    reduce_sum x2, other arithmetic, layer_norm(): center = values - jnp.mean(values, axis=-1, keepdims=True)  7.28 us
    dot_general x1, matrix products, section_compute(): jnp.dot(columns, lax.all_gather(qkv_rows, 'sess', axis=0, tiled=True), pr...  6.66 us
    unnamed x25, local copies, waits for them, and re-layouts  6.01 us
    another operation x4, other arithmetic, body(): picks.append(jnp.argmax(target_device == wanted))  5.47 us
  transfers between devices with their start and end apart: 11, of which 3 were waited for; matrix products, arithmetic and copies ran while one was open for 24% of the time, Pallas kernels for 0%

commit v1 on v0

v1 whole, which is shorter than its diff:
```python
import functools

import jax
import jax.numpy as jnp
from jax import lax
from jax.experimental import pallas as pl
from jax.experimental.pallas import tpu as pltpu
from jax.sharding import PartitionSpec as P

D = 1536
HEADS = 8
HSIZE = 96
HD = 768
KERNEL = 31
EDGE = 30
CTX = 64
FR = 16
SLOTS = 12
RING = 8
N_SESS = 128
QW = 3 * HD
N0 = 1152
N1 = QW - N0
WIDTHS = (N0, N1)
STARTS = (0, N0)
OH = D // 2
OFFSETS = (1, -1, 2, -2)
MESH = pl.DeviceIdType.MESH
F32 = jnp.float32
BF16 = jnp.bfloat16


class Ring:
    def __init__(self, slot, me, plus, minus, send, recv, parts):
        self.slot, self.me, self.ids = slot, me, (plus, minus)
        self.send, self.recv, self.parts = send, recv, parts

    def hops(self, d, h):
        if self.parts == 1:
            return 4 - d
        return 4 if d == h else 3

    def group(self, d, k):
        return lax.rem(self.me + (RING - k if d == 0 else k), RING)

    def index(self, d, h, k):
        return (d * self.parts + h) * 4 + k - 1

    def copy(self, d, h, k, back):
        ref = self.slot(self.group(d, k - back), h)
        at = self.index(d, h, k)
        return pltpu.make_async_remote_copy(
            src_ref=ref,
            dst_ref=ref,
            send_sem=self.send.at[at],
            recv_sem=self.recv.at[at],
            device_id=self.ids[d],
            device_id_type=MESH,
        )

    def start(self):
        for h in range(self.parts):
            for d in ((0, 1) if h == 0 else (1, 0)):
                self.copy(d, h, 1, 1).start()

    def arrive(self, d, h, k):
        if k > self.hops(d, h):
            return False
        self.copy(d, h, k, 0).wait_recv()
        if k < self.hops(d, h):
            self.copy(d, h, k + 1, 1).start()
        return True

    def drain(self):
        for h in range(self.parts):
            for d in range(2):
                for k in range(1, self.hops(d, h) + 1):
                    self.copy(d, h, k, 1).wait_send()


def share_index(d, h, k):
    return h if k == 0 else 2 + (d * 2 + h) * 4 + k - 1


def every_share():
    out = [(0, 0, 0), (0, 1, 0)]
    for d in range(2):
        for h in range(2):
            for k in range(1, (4 if d == h else 3) + 1):
                out.append((d, h, k))
    return out


def layer_norm(values, gain):
    center = values - jnp.mean(values, axis=-1, keepdims=True)
    spread = jnp.mean(center * center, axis=-1, keepdims=True)
    return center * lax.rsqrt(spread + 1e-05) * gain


def kernel(
    frames, edges, cache, gains, taps, wq, wo, targets, lengths, counts,
    out,
    e_loc, c_loc, e_stage, c_stage, e_arr, c_arr,
    x_q0, x_q1, x_o, bufq0, bufq1, p1o, bufo,
    tmp_q, tmp_o, seq, mid, second, proj, ctx, hmask, ostage,
    loc_sem, x_send, x_recv, m_send, m_recv,
    pq_send, pq_recv, po_send, po_recv,
    qq_send, qq_recv, qo_send, qo_recv,
    sq_send, sq_recv, so_send, so_recv,
    h_send, h_recv,
):
    sess = lax.axis_index("sess")
    sec = lax.axis_index("section")
    nsec = lax.axis_size("section")
    core = lax.rem(sess, 2)
    chip = sess // 2
    y = lax.rem(chip, RING)
    z = chip // RING

    def at(zz, yy, cc):
        return ((zz * RING + yy) * 2 + cc, sec)

    def step(v, by):
        return lax.rem(v + RING + by, RING)

    sib = at(z, y, 1 - core)
    y_ids = (at(z, step(y, 1), core), at(z, step(y, -1), core))
    z_ids = (at(step(z, 1), y, core), at(step(z, -1), y, core))
    next_sec = (sess, lax.rem(sec + 1, nsec))
    prev_sec = (sess, lax.rem(sec + nsec - 1, nsec))
    moves = [(lax.rem(sess + N_SESS + o, N_SESS), sec) for o in OFFSETS]
    bufq = (bufq0, bufq1)
    x_q = (x_q0, x_q1)

    def by_role(fn):
        for role in range(2):
            @pl.when(core == role)
            def _():
                fn(role)

    load_e = pltpu.make_async_copy(edges, e_loc, loc_sem.at[0])
    load_c = pltpu.make_async_copy(cache, c_loc, loc_sem.at[1])
    load_e.start()
    load_c.start()

    barrier = pltpu.get_barrier_semaphore()
    greet = [*moves, *y_ids, *z_ids, sib, next_sec, prev_sec]
    for dev in greet:
        pl.semaphore_signal(barrier, inc=1, device_id=dev, device_id_type=MESH)

    wanted = [m[0] * SLOTS for m in moves]

    def hits(j):
        t = targets[j]
        return [(t >= w) & (t < w + SLOTS) for w in wanted]

    picks = [jnp.int32(0)] * 4
    for j in range(SLOTS):
        picks = [jnp.where(hit, jnp.int32(j), p) for hit, p in zip(hits(j), picks)]

    def source(j):
        found = hits(j)
        arrived = found[0] | found[1] | found[2] | found[3]
        place = jnp.int32(0)
        for r in range(1, 4):
            place = jnp.where(found[r], jnp.int32(r), place)
        return arrived, place

    def pick(arrived, there, here):
        return jnp.where(arrived, there, here)

    pl.semaphore_wait(barrier, len(greet))

    def swap_q(role, dst_role):
        return pltpu.make_async_remote_copy(
            src_ref=wq.at[:, pl.ds(STARTS[dst_role], WIDTHS[dst_role])],
            dst_ref=x_q[dst_role],
            send_sem=x_send.at[0],
            recv_sem=x_recv.at[0],
            device_id=sib,
            device_id_type=MESH,
        )

    def swap_o(role):
        return pltpu.make_async_remote_copy(
            src_ref=wo.at[:, pl.ds((1 - role) * OH, OH)],
            dst_ref=x_o,
            send_sem=x_send.at[1],
            recv_sem=x_recv.at[1],
            device_id=sib,
            device_id_type=MESH,
        )

    def start_swap(role):
        swap_q(role, 1 - role).start()
        swap_o(role).start()

    by_role(start_swap)

    def migrate(r, stage, arr, base):
        return pltpu.make_async_remote_copy(
            src_ref=stage.at[r],
            dst_ref=arr.at[r],
            send_sem=m_send.at[base + r],
            recv_sem=m_recv.at[base + r],
            device_id=moves[r],
            device_id_type=MESH,
        )

    load_e.wait()
    for r in range(4):
        e_stage[r] = e_loc[picks[r]]
        migrate(r, e_stage, e_arr, 0).start()

    def q_slot_block(role):
        if role == 0:
            return lambda g, h: bufq0.at[z, g]
        return lambda g, h: bufq1.at[g, y]

    def q_slot_group(role):
        if role == 0:
            return lambda g, h: bufq0.at[g, pl.ds(4 * h, 4)]
        return lambda g, h: bufq1.at[pl.ds(4 * h, 4), g]

    def ring_pq(role):
        me, ids = ((y, y_ids), (z, z_ids))[role]
        return Ring(q_slot_block(role), me, *ids, pq_send, pq_recv, 1)

    def ring_qq(role):
        me, ids = ((z, z_ids), (y, y_ids))[role]
        return Ring(q_slot_group(role), me, *ids, qq_send, qq_recv, 2)

    ring_po = Ring(lambda g, h: p1o.at[g], y, *y_ids, po_send, po_recv, 1)
    ring_qo = Ring(
        lambda g, h: bufo.at[core, g, pl.ds(48 * h, 48)], z, *z_ids, qo_send, qo_recv, 2
    )

    def enter_q(role):
        n = WIDTHS[role]
        swap_q(role, role).wait_recv()
        own = wq[:, STARTS[role]:STARTS[role] + n].astype(F32)
        other = x_q[role][...].astype(F32)
        if role == 0:
            tmp_q[0:12, 0:n] = own
            tmp_q[12:24, 0:n] = other
        else:
            tmp_q[0:12, 0:n] = other
            tmp_q[12:24, 0:n] = own
        bufq[role][z, y] = tmp_q[:, 0:n].astype(BF16)
        ring_pq(role).start()

    by_role(enter_q)

    def enter_o(role):
        swap_o(role).wait_recv()
        own = wo[:, role * OH:(role + 1) * OH].astype(F32)
        other = x_o[...].astype(F32)
        first, last = (own, other) if role == 0 else (other, own)
        tmp_o[0:6, :] = first
        tmp_o[6:12, :] = last

    by_role(enter_o)
    p1o[y] = tmp_o[0:12, :].astype(BF16)
    ring_po.start()

    head_of_row = lax.broadcasted_iota(jnp.int32, (HEADS * FR, HD), 0) // FR
    lane = lax.broadcasted_iota(jnp.int32, (HEADS * FR, HD), 1)
    inside = (lane >= head_of_row * HSIZE) & (lane < head_of_row * HSIZE + HSIZE)
    hmask[...] = jnp.where(inside, 1.0, 0.0).astype(BF16)
    load_c.wait()
    for r in range(4):
        c_stage[r] = c_loc[picks[r]]

    for k in range(1, 5):
        def go(role):
            ring = ring_pq(role)
            ring.arrive(0, 0, k)
            ring.arrive(1, 0, k)
        by_role(go)
        ring_po.arrive(0, 0, k)
        ring_po.arrive(1, 0, k)

    def share(role, d, h, k, q):
        if q:
            ring = ring_qq(role)
            sems = (sq_send, sq_recv)
        else:
            ring = ring_qo
            sems = (so_send, so_recv)
        ref = ring.slot(ring.group(d, k), h)
        i = share_index(d, h, k)
        return pltpu.make_async_remote_copy(
            src_ref=ref,
            dst_ref=ref,
            send_sem=sems[0].at[i],
            recv_sem=sems[1].at[i],
            device_id=sib,
            device_id_type=MESH,
        )

    def start_qq(role):
        ring_qq(role).start()
        share(role, 0, 0, 0, True).start()
        share(role, 0, 1, 0, True).start()

    by_role(start_qq)
    for r in range(4):
        migrate(r, c_stage, c_arr, 4).start()

    for p in range(RING):
        tmp_o[12 * p:12 * p + 12, :] = p1o[p].astype(F32)
    bufo[core, z] = tmp_o[...].astype(BF16)

    def start_qo():
        ring_qo.start()
        share(0, 0, 0, 0, False).start()
        share(0, 0, 1, 0, False).start()

    def serve_q(h, k):
        def go(role):
            ring = ring_qq(role)
            for d in ((0, 1) if h == 0 else (1, 0)):
                if ring.arrive(d, h, k):
                    share(role, d, h, k, True).start()
        by_role(go)

    def serve_o(k):
        for h in range(2):
            for d in range(2):
                if ring_qo.arrive(d, h, k):
                    share(0, d, h, k, False).start()

    for r in range(4):
        migrate(r, e_stage, e_arr, 0).wait_recv()

    def front(j, carry):
        x = frames[j].astype(F32)
        normed = layer_norm(x, gains[0:1, :]).astype(BF16)
        arrived, place = source(j)
        seq[0:EDGE, :] = pick(arrived, e_arr[place], e_loc[j]).astype(F32)
        seq[EDGE:EDGE + FR, :] = normed.astype(F32)
        rows = pl.ds(pl.multiple_of(j * FR, FR), FR)
        for c in range(D // 128):
            lanes = slice(128 * c, 128 * c + 128)
            total = taps[0:1, lanes] * seq[0:FR, lanes]
            for t in range(1, KERNEL):
                total = total + taps[t:t + 1, lanes] * seq[t:t + FR, lanes]
            mid[rows, lanes] = frames[j, :, lanes].astype(F32) + total
        second[rows, :] = layer_norm(mid[rows, :], gains[1:2, :]).astype(BF16)
        return carry

    for k in range(1, 4):
        for h in range(2):
            i = 2 * ((k - 1) * 2 + h)
            lax.fori_loop(i, i + 2, front, 0)
            serve_q(h, k)
    start_qo()
    serve_q(0, 4)
    serve_q(1, 4)

    def shared_q(role):
        for d, h, k in every_share():
            share(1 - role, d, h, k, True).wait_recv()

    by_role(shared_q)

    for role in range(2):
        n = WIDTHS[role]
        total = jnp.zeros((SLOTS * FR, n), F32)
        for g in range(4):
            part = bufq[role][2 * g:2 * g + 2].astype(F32).reshape(384, n).astype(BF16)
            total = total + jnp.dot(
                second[:, 384 * g:384 * g + 384], part, preferred_element_type=F32
            )
        proj[:, STARTS[role]:STARTS[role] + n] = total.astype(BF16)
        serve_o(1 + role)

    for r in range(4):
        migrate(r, c_stage, c_arr, 4).wait_recv()

    key_pos = lax.broadcasted_iota(jnp.int32, (HEADS * FR, CTX + FR), 1)
    frame = lax.rem(lax.broadcasted_iota(jnp.int32, (HEADS * FR, CTX + FR), 0), FR)

    def attend(j, carry):
        rows = pl.ds(pl.multiple_of(j * FR, FR), FR)
        arrived, place = source(j)
        cached = pick(arrived, c_arr[place], c_loc[j])
        keys = jnp.concatenate([cached[:, :HD], proj[rows, HD:2 * HD]], axis=0)
        values = jnp.concatenate([cached[:, HD:], proj[rows, 2 * HD:]], axis=0)
        q = proj[rows, :HD]
        queries = jnp.concatenate([q] * HEADS, axis=0) * hmask[...]
        scores = lax.dot_general(
            queries, keys, (((1,), (1,)), ((), ())), preferred_element_type=F32
        ) * HSIZE ** (-0.5)
        allowed = ((key_pos < CTX) & (key_pos >= CTX - lengths[j])) | (
            (key_pos >= CTX) & (key_pos - CTX <= frame)
        )
        scores = jnp.where(allowed, scores, -1e30)
        weights = jnp.exp(scores - jnp.max(scores, axis=-1, keepdims=True))
        probs = (weights / jnp.sum(weights, axis=-1, keepdims=True)).astype(BF16)
        wide = jnp.dot(probs, values, preferred_element_type=F32)
        wide = wide * hmask[...].astype(F32)
        total = wide[0:FR]
        for hd in range(1, HEADS):
            total = total + wide[FR * hd:FR * hd + FR]
        ctx[rows, :] = total.astype(BF16)
        return carry

    lax.fori_loop(0, 6, attend, 0)
    serve_o(3)
    lax.fori_loop(6, SLOTS, attend, 0)
    serve_o(4)

    def shared_o(role):
        for d, h, k in every_share():
            i = share_index(d, h, k)
            ref = bufo.at[1 - core, ring_qo.group(d, k), pl.ds(48 * h, 48)]
            pltpu.make_async_remote_copy(
                src_ref=ref,
                dst_ref=ref,
                send_sem=so_send.at[i],
                recv_sem=so_recv.at[i],
                device_id=sib,
                device_id_type=MESH,
            ).wait_recv()

    shared_o(0)

    def hand(n):
        lanes = pl.ds(384 * n, 384)
        return pltpu.make_async_remote_copy(
            src_ref=ostage.at[:, :, lanes],
            dst_ref=out.at[:, :, lanes],
            send_sem=h_send.at[n],
            recv_sem=h_recv.at[n],
            device_id=next_sec,
            device_id_type=MESH,
        )

    for n in range(4):
        lanes = slice(384 * n, 384 * n + 384)
        half, at_lane = n // 2, 384 * (n % 2)
        weights = bufo[half, :, :, at_lane:at_lane + 384].reshape(HD, 384)
        result = jnp.dot(ctx[...], weights, preferred_element_type=F32) + mid[:, lanes]
        for j in range(SLOTS):
            live = counts[0] > j
            ostage[j, :, lanes] = jnp.where(
                live, result[FR * j:FR * j + FR], 0.0
            ).astype(BF16)
        hand(n).start()

    def drain_role(role):
        swap_q(role, 1 - role).wait_send()
        swap_o(role).wait_send()
        ring_pq(role).drain()
        ring_qq(role).drain()
        for d, h, k in every_share():
            share(role, d, h, k, True).wait_send()

    by_role(drain_role)
    ring_po.drain()
    ring_qo.drain()
    for d, h, k in every_share():
        share(0, d, h, k, False).wait_send()
    for r in range(4):
        migrate(r, e_stage, e_arr, 0).wait_send()
        migrate(r, c_stage, c_arr, 4).wait_send()
    for n in range(4):
        hand(n).wait_send()
        hand(n).wait_recv()


def body(
    new_frames, conv_edges, kv_cache, norm_gains, conv_kernel,
    w_qkv, w_out, move_targets, lengths, counts,
):
    vmem = pl.BlockSpec(memory_space=pltpu.VMEM)
    smem = pl.BlockSpec(memory_space=pltpu.SMEM)
    any_ = pl.BlockSpec(memory_space=pl.ANY)
    dma = pltpu.SemaphoreType.DMA
    rows = SLOTS * FR
    out = pl.pallas_call(
        kernel,
        out_shape=jax.ShapeDtypeStruct((SLOTS, FR, D), BF16),
        in_specs=[vmem, any_, any_, vmem, vmem, vmem, vmem, smem, smem, smem],
        out_specs=any_,
        scratch_shapes=[
            pltpu.VMEM((SLOTS, EDGE, D), BF16),
            pltpu.VMEM((SLOTS, CTX, D), BF16),
            pltpu.VMEM((4, EDGE, D), BF16),
            pltpu.VMEM((4, CTX, D), BF16),
            pltpu.VMEM((4, EDGE, D), BF16),
            pltpu.VMEM((4, CTX, D), BF16),
            pltpu.VMEM((12, N0), BF16),
            pltpu.VMEM((12, N1), BF16),
            pltpu.VMEM((6, OH), BF16),
            pltpu.VMEM((RING, RING, 24, N0), BF16),
            pltpu.VMEM((RING, RING, 24, N1), BF16),
            pltpu.VMEM((RING, 12, OH), BF16),
            pltpu.VMEM((2, RING, 96, OH), BF16),
            pltpu.VMEM((24, max(N0, N1)), F32),
            pltpu.VMEM((96, OH), F32),
            pltpu.VMEM((48, D), F32),
            pltpu.VMEM((rows, D), F32),
            pltpu.VMEM((rows, D), BF16),
            pltpu.VMEM((rows, QW), BF16),
            pltpu.VMEM((rows, HD), BF16),
            pltpu.VMEM((HEADS * FR, HD), BF16),
            pltpu.VMEM((SLOTS, FR, D), BF16),
            dma((2,)), dma((2,)), dma((2,)), dma((8,)), dma((8,)),
            dma((8,)), dma((8,)), dma((8,)), dma((8,)),
            dma((16,)), dma((16,)), dma((16,)), dma((16,)),
            dma((18,)), dma((18,)), dma((18,)), dma((18,)),
            dma((4,)), dma((4,)),
        ],
        compiler_params=pltpu.CompilerParams(
            collective_id=0, has_side_effects=True, vmem_limit_bytes=56 * 2 ** 20
        ),
        cost_estimate=pl.CostEstimate(
            flops=2 * 10 ** 9, bytes_accessed=6 * 10 ** 6, transcendentals=10 ** 5
        ),
    )(
        new_frames[0], conv_edges[0], kv_cache[0], norm_gains[0], conv_kernel[0],
        w_qkv[0], w_out[0], move_targets, lengths, counts,
    )
    return out[None]


def solution(mesh):
    placed = (
        P("section", "sess", None, None),
        P("section", "sess", None, None),
        P("section", "sess", None, None),
        P("section", None, None),
        P("section", None, None),
        P("section", "sess", None),
        P("section", "sess", None),
        P("sess"),
        P("sess"),
        P("sess"),
    )
    return jax.shard_map(
        body,
        mesh=mesh,
        in_specs=placed,
        out_specs=P("section", "sess", None, None),
        check_vma=False,
    )
```

time: 227 us -> 101 us (0.44)
  waiting for transfers between devices: 99 us -> 0 us
  Pallas kernels: 0 us -> 96.3 us
  starting transfers between devices: 41.9 us -> 0 us
  other arithmetic: 25.8 us -> 0 us
  between operations: 21.9 us -> 0.66 us
  matrix products: 17.2 us -> 0 us
  local copies, waits for them, and re-layouts: 20 us -> 3.53 us
    pallas_call x0 -> x1, Pallas kernels: none -> 96.3 us  [body(): pl.pallas_call(kernel, out_shape=jax.ShapeDtypeStruct((SLOTS, FR, D), BF1...]
    all_gather x2 -> x0, waiting for transfers between devices: 84.3 us -> none  [the longest x1 57.2 us: section_compute(): lax.all_gather(out_rows, 'sess', axis=0, tiled=True)]
    ppermute x9 -> x0, starting transfers between devices: 41.8 us -> none  [passed_along(): return lax.ppermute(x, axis, [(i, (i + by) % size) for i in range(size)])]
    dot_general x4 -> x0, matrix products: 17.2 us -> none  [the longest x1 6.66 us: section_compute(): jnp.dot(columns, lax.all_gather(qkv_rows, 'sess', axis=0, tiled=True), pr...]
    ppermute x9 -> x0, waiting for transfers between devices: 14.7 us -> none  [passed_along(): return lax.ppermute(x, axis, [(i, (i + by) % size) for i in range(size)])]
    reshape x3 -> x0, local copies, waits for them, and re-layouts: 8.11 us -> none  [the longest x1 3.59 us: attend(): key_heads = keys.reshape(session_count, CTX + FR, HEADS, HSIZE)]
    reduce_sum x4 -> x0, other arithmetic: 7.84 us -> none  [the longest x2 7.28 us: layer_norm(): center = values - jnp.mean(values, axis=-1, keepdims=True)]
    scatter x8 -> x0, other arithmetic: 6.98 us -> none  [the longest x4 4.34 us: body(): moved_edges = moved_edges.at[slot_pick].set(arrived[0])]
  transfers between devices with their start and end apart: 11 -> 0, of which waited for: 3 -> 0; matrix products, arithmetic and copies ran while one was open for 24% -> 0% of each run, Pallas kernels for 0% -> 0%
where the time goes in v1:
time: 101 us
  Pallas kernels  96.3 us (95%)
  local copies, waits for them, and re-layouts  3.53 us (3%)
    pallas_call x1, Pallas kernels, body(): pl.pallas_call(kernel, out_shape=jax.ShapeDtypeStruct((SLOTS, FR, D), BF1...  96.3 us
    unnamed x2, local copies, waits for them, and re-layouts  3.53 us

profile of v1, /device:TPU:1, one launch (start us, length us, event | category | flops | bytes accessed | tf_op | source)
XLA Modules:
  0.0 100.5 jit_solution(16189855439683492252)
XLA Ops:
  0.7 1.6 %copy.13 = f32[1,31,1536]{2,1,0:T(8,128)} copy(f32[1,31,1536]{2,0,1:T(1,128)} %param.14) | data formatting | bytes 380928
  2.3 96.3 %shard_map.100 = bf16[12,16,1536]{2,1,0:T(8,128)(2,1)} custom-call(bf16[12,16,1536]{2,1,0:T(8,128)(2,1)} %bitcast.14, bf16[12,30,1536]{2,1,0:T(8,128)(2,1)} %bitcast.13, bf16[12,64,1536]{2,1,0:T(8,128)(2,1)} %bitcast.12, f32[2,1536]{1,0:T(2,128)} %bitcast.17, f32[31,1536]{1,0:T(8,128)} %bitcast.11, bf16[12,2304]{1,0:T(8,128)(2,1)} %bitcast.15, ...), custom_call_target="tpu_custom_call" | custom-call | flops 2000000000 | bytes 6000000 | tf_op jit(solution)/shard_map/pallas_call | solution.py:482
  98.6 1.9 %copy.16 = bf16[1,12,16,1536]{3,2,1,0:T(8,128)(2,1)} copy(bf16[1,12,16,1536]{3,2,1,0:T(8,128)(2,1)} %bitcast.10) | data formatting | bytes 1179648

commit v2 on v0

v2 whole, which is shorter than its diff:
```python
import functools

import jax
import jax.numpy as jnp
from jax import lax
from jax.experimental import pallas as pl
from jax.experimental.pallas import tpu as pltpu
from jax.sharding import PartitionSpec as P

D = 1536
HEADS = 8
HSIZE = 96
HD = 768
KERNEL = 31
EDGE = 30
CTX = 64
FR = 16
SLOTS = 12
RING = 8
N_SESS = 128
QW = 3 * HD
OH = D // 2
WIDTHS = (2 * HD, HD)
STARTS = (0, 2 * HD)
PART = HD // 2
GROUP = 4
LAST = RING - 1
TILES = ((0, 3), (2, 6), (5, 8))
TILE_ROWS = ((0, 48), (48, 112), (112, 160))
OFFSETS = (1, -1, 2, -2)
MESH = pl.DeviceIdType.MESH
F32 = jnp.float32
BF16 = jnp.bfloat16


class Book:
    def __init__(self):
        self.started, self.arrived, self.left = {}, set(), set()

    def start(self, role, make, key):
        make().start()
        self.started[(role, key)] = make

    def arrive(self, role, make, key):
        make().wait_recv()
        self.arrived.add((role, key))

    def sent(self, role, key):
        self.started[(role, key)]().wait_send()
        self.left.add((role, key))

    def close(self, role):
        for key, make in self.started.items():
            if key[0] == role and key not in self.left:
                make().wait_send()
            if key[0] == role and key not in self.arrived:
                make().wait_recv()


def hops(d, h):
    return 4 if d == h else 3


def turn(me, by):
    return lax.rem(me + (by % RING), RING)


def every_share():
    out = [(0, 0, 0), (0, 1, 0)]
    for d in range(2):
        for h in range(2):
            for k in range(1, hops(d, h) + 1):
                out.append((d, h, k))
    return out


def remote(src, dst, send, recv, i, dev):
    return pltpu.make_async_remote_copy(
        src_ref=src,
        dst_ref=dst,
        send_sem=send.at[i],
        recv_sem=recv.at[i],
        device_id=dev,
        device_id_type=MESH,
    )


class Spread:
    def __init__(self, book, role, name, slot, me, ids, sems):
        self.book, self.role, self.name = book, role, name
        self.slot, self.me, self.ids, self.sems = slot, me, ids, sems

    def copy(self, d, h, back):
        ref = self.slot(turn(self.me, back), h)
        return remote(ref, ref, *self.sems, 8 * h + d - 1, self.ids(d))

    def start(self, h):
        for d in (1, 7, 2, 6, 3, 5, 4):
            make = lambda d=d: self.copy(d, h, 0)
            self.book.start(self.role, make, (self.name, d, h))

    def arrive(self, h):
        for d in (1, 7, 2, 6, 3, 5, 4):
            self.book.arrive(self.role, lambda: self.copy(d, h, -d), (self.name, d, h))


class Ring:
    def __init__(self, book, role, name, slot, me, place, away, sib, sems, share_sems):
        self.book, self.role, self.name = book, role, name
        self.slot, self.me, self.place, self.away = slot, me, place, away
        self.sib, self.sems, self.share_sems = sib, sems, share_sems

    def group(self, d, k):
        return turn(self.me, -k if d == 0 else k)

    def copy(self, d, h, k, back):
        ref = self.slot(self.group(d, k - back), h)
        to = self.place(turn(self.me, 1 - 2 * d))
        return remote(ref, ref, *self.sems, (d * 2 + h) * 4 + k - 1, to)

    def last(self, h, back):
        away = self.away[h]
        group = lax.rem(self.me + 5 + 6 * away, RING) if back else turn(self.me, 4)
        ref = self.slot(group, h)
        to = self.place(lax.rem(self.me + 1 + 6 * away, RING))
        return remote(ref, ref, *self.sems, 12 * h + 3, to)

    def share(self, d, h, k):
        ref = self.slot(self.group(d, k), h)
        i = h if k == 0 else 2 + (d * 2 + h) * 4 + k - 1
        return remote(ref, ref, *self.share_sems, i, self.sib)

    def pass_on(self, d, h, k):
        make = lambda: self.copy(d, h, k + 1, 1)
        self.book.start(self.role, make, (self.name, d, h, k + 1))

    def give(self, d, h, k):
        self.book.start(self.role, lambda: self.share(d, h, k), (self.name, "s", d, h, k))

    def start(self, h):
        for d in (h, 1 - h):
            self.pass_on(d, h, 0)
        self.give(0, h, 0)

    def serve(self, h, k):
        if k == 4:
            self.book.arrive(self.role, lambda: self.last(h, 0), (self.name, h, h, 4))
            self.give(h, h, 4)
            return
        for d in (h, 1 - h):
            self.book.arrive(self.role, lambda: self.copy(d, h, k, 0), (self.name, d, h, k))
            if k < 3:
                self.pass_on(d, h, k)
                self.give(d, h, k)
        if k == 3:
            make = lambda: self.last(h, 1)
            self.book.start(self.role, make, (self.name, h, h, 4))
            for d in (h, 1 - h):
                self.give(d, h, k)

    def shared(self, book_role, parts=(0, 1)):
        for d, h, k in every_share():
            if h in parts:
                self.book.arrive(book_role, lambda: self.share(d, h, k), (self.name, "s", d, h, k))


def layer_norm(values, gain):
    center = values - jnp.mean(values, axis=-1, keepdims=True)
    spread = jnp.mean(center * center, axis=-1, keepdims=True)
    return center * lax.rsqrt(spread + 1e-05) * gain


def kernel(
    frames_in, edges, cache, gains, taps_in, wq_in, wo_in, targets, lengths, counts,
    out,
    frames, taps, wq, wo,
    e_loc, c_loc, e_stage, c_stage, e_arr, c_arr, e_via, c_via,
    x_q0, x_q1, x_o, bufq0, bufq1, p1o, bufo,
    tmp_q, tmp_o, seq, mid, second, proj, ctx, hmask, fmask, order, ostage,
    loc_sem, x_send, x_recv, m_send, m_recv,
    pq_send, pq_recv, po_send, po_recv,
    qq_send, qq_recv, qo_send, qo_recv,
    sq_send, sq_recv, so_send, so_recv,
    h_send, h_recv, v_send, v_recv,
):
    sess = lax.axis_index("sess")
    sec = lax.axis_index("section")
    nsec = lax.axis_size("section")
    core = lax.rem(sess, 2)
    y = lax.rem(sess // 2, RING)
    z = sess // (2 * RING)
    book = Book()

    def at(zz, yy, cc):
        return ((zz * RING + yy) * 2 + cc, sec)

    def on_y(d):
        return at(z, turn(y, d), core)

    def on_z(d):
        return at(turn(z, d), y, core)

    sib = at(z, y, 1 - core)
    next_sec = (sess, lax.rem(sec + 1, nsec))
    prev_sec = (sess, lax.rem(sec + nsec - 1, nsec))
    moves = [(lax.rem(sess + N_SESS + o, N_SESS), sec) for o in OFFSETS]
    bufq = (bufq0, bufq1)
    x_q = (x_q0, x_q1)

    def by_role(fn):
        for role in range(2):
            @pl.when(core == role)
            def _():
                fn(role)

    barrier = pltpu.get_barrier_semaphore()
    greet = [*moves, sib, next_sec, prev_sec, at(z, LAST - y, 1 - core)]
    greet += [on_y(d) for d in range(1, RING)] + [on_z(d) for d in range(1, RING)]
    for dev in greet:
        pl.semaphore_signal(barrier, inc=1, device_id=dev, device_id_type=MESH)

    loads = [
        pltpu.make_async_copy(src, dst, loc_sem.at[i])
        for i, (src, dst) in enumerate(
            ((wq_in, wq), (wo_in, wo), (edges, e_loc), (cache, c_loc),
             (frames_in, frames), (taps_in, taps))
        )
    ]
    for load in loads:
        load.start()

    wanted = [m[0] * SLOTS for m in moves]

    def hits(j):
        t = targets[j]
        return [(t >= w) & (t < w + SLOTS) for w in wanted]

    picks = [jnp.int32(0)] * 4
    for j in range(SLOTS):
        picks = [jnp.where(hit, jnp.int32(j), p) for hit, p in zip(hits(j), picks)]

    def source(j):
        found = hits(j)
        arrived = found[0] | found[1] | found[2] | found[3]
        place = jnp.int32(0)
        for r in range(1, 4):
            place = jnp.where(found[r], jnp.int32(r), place)
        return arrived, place

    for load in loads[:3]:
        load.wait()
    pl.semaphore_wait(barrier, len(greet))

    def swap_q(dst_role):
        return remote(
            wq.at[:, pl.ds(STARTS[dst_role], WIDTHS[dst_role])],
            x_q[dst_role], x_send, x_recv, 0, sib,
        )

    def swap_o(role):
        return remote(wo.at[:, pl.ds((1 - role) * OH, OH)], x_o, x_send, x_recv, 1, sib)

    def start_swap(role):
        book.start(role, lambda: swap_q(1 - role), "xq")
        book.start(role, lambda: swap_o(role), "xo")

    by_role(start_swap)

    def copy_e(r):
        return remote(e_stage.at[r], e_arr.at[r], m_send, m_recv, r, moves[r])

    def copy_c(r):
        return remote(c_stage.at[r], c_arr.at[r], m_send, m_recv, 4 + r, moves[r])

    crossing = [(y == LAST) & (core == 1), (y == 0) & (core == 0), y == LAST, y == 0]
    parts = ((e_stage, e_via, e_arr), (c_stage, c_via, c_arr))

    def across_z(m, r):
        stage, via, _ = parts[m]
        i = 2 * m + r // 2
        return remote(
            stage.at[r], via.at[r // 2], v_send, v_recv, i, on_z(1 if r % 2 == 0 else -1)
        )

    def along_y(m, r):
        _, via, arr = parts[m]
        to = at(z, LAST - y, core if r >= 2 else 1 - core)
        return remote(via.at[r // 2], arr.at[r], m_send, m_recv, 4 * m + r, to)

    def leave_row(m):
        for r in range(4):
            @pl.when(crossing[r])
            def _():
                book.start(("z", r), lambda r=r: across_z(m, r), ("z", m))

    def leave(m):
        for r in range(4):
            @pl.when(jnp.logical_not(crossing[r]))
            def _():
                book.start(("d", r), lambda r=r: (copy_e, copy_c)[m](r), ("d", m))
                book.arrived.add((("d", r), ("d", m)))

    def pass_along(m):
        for r in range(4):
            @pl.when(crossing[r])
            def _():
                book.arrive(("z", r), lambda r=r: across_z(m, r), ("z", m))
                book.start(("z", r), lambda r=r: along_y(m, r), ("y", m))
                book.arrived.add((("z", r), ("y", m)))

    for r in range(4):
        e_stage[r] = e_loc[picks[r]]
    leave_row(0)
    loads[3].wait()
    for r in range(4):
        c_stage[r] = c_loc[picks[r]]
    leave_row(1)

    def q_block(role):
        if role == 0:
            return lambda g, h: bufq0.at[h, z, g]
        return lambda g, h: bufq1.at[h, g, y]

    def q_group(role):
        if role == 0:
            return lambda g, h: bufq0.at[h, g]
        return lambda g, h: bufq1.at[h, :, g]

    along, across = (y, z), (z, y)
    on_along = (on_y, on_z)
    across_at = (lambda v: at(v, y, core), lambda v: at(z, v, core))
    away = ((0, 1), (0, 1))
    spread_q = [
        Spread(book, role, "pq", q_block(role), along[role], on_along[role],
               (pq_send, pq_recv))
        for role in range(2)
    ]
    ring_q = [
        Ring(book, role, "qq", q_group(role), across[role], across_at[role], away[role], sib,
             (qq_send, qq_recv), (sq_send, sq_recv))
        for role in range(2)
    ]
    spread_o = [
        Spread(book, role, "po", lambda g, h: p1o.at[g], along[role], on_along[role],
               (po_send, po_recv))
        for role in range(2)
    ]
    ring_o = [
        Ring(book, role, "qo", lambda g, h, role=role: bufo.at[role, h, g], across[role],
             across_at[role], away[role], sib, (qo_send, qo_recv), (so_send, so_recv))
        for role in range(2)
    ]

    def joined(role, n, own, other):
        first, last = (own, other) if role == 0 else (other, own)
        return first.astype(F32), last.astype(F32)

    def enter_q(role):
        book.arrive(role, lambda: swap_q(role), "xq")
        width = WIDTHS[role] // 2
        for h in range(2):
            for m in range(0, width, PART):
                lanes = slice(2 * m + PART * h, 2 * m + PART * h + PART)
                own = wq[:, STARTS[role] + lanes.start:STARTS[role] + lanes.stop]
                first, last = joined(role, 12, own, x_q[role][:, lanes])
                tmp_q[0:12, m:m + PART] = first
                tmp_q[12:24, m:m + PART] = last
            bufq[role][h, z, y] = tmp_q[:, 0:width].astype(BF16)
            spread_q[role].start(h)

    by_role(enter_q)
    leave(0)

    def enter_o(role):
        book.arrive(role, lambda: swap_o(role), "xo")
        first, last = joined(role, 6, wo[:, role * OH:(role + 1) * OH], x_o[...])
        tmp_o[0:6, :] = first
        tmp_o[6:12, :] = last
        p1o[along[role]] = tmp_o[0:12, :].astype(BF16)

    by_role(enter_o)

    for (low, high), (top, end) in zip(TILES, TILE_ROWS):
        shape = (end - top, 256)
        head = lax.broadcasted_iota(jnp.int32, shape, 0) // FR + low
        lane = lax.broadcasted_iota(jnp.int32, shape, 1) + 256 * TILES.index((low, high))
        inside = (lane >= head * HSIZE) & (lane < head * HSIZE + HSIZE)
        fmask[top:end, :] = jnp.where(inside, 1.0, 0.0)
        hmask[top:end, :] = jnp.where(inside, 1.0, 0.0).astype(BF16)
    for load in loads[4:]:
        load.wait()

    def start_q(role):
        for h in range(2):
            spread_q[role].arrive(h)
            ring_q[role].start(h)
        spread_o[role].start(0)

    by_role(start_q)
    pass_along(0)
    leave(1)
    pass_along(1)

    for i in range(HD // 128):
        shape = (HD, 128)
        to = lax.broadcasted_iota(jnp.int32, shape, 1) + 128 * i
        by_y, rest = to // 96, lax.rem(to, 96)
        source_row = (rest // 12) * 96 + by_y * 12 + lax.rem(rest, 12)
        same = lax.broadcasted_iota(jnp.int32, shape, 0) == source_row
        order[:, 128 * i:128 * i + 128] = jnp.where(same, 1.0, 0.0).astype(BF16)
    def front(j, carry):
        x = frames[j].astype(F32)
        normed = layer_norm(x, gains[0:1, :]).astype(BF16)
        arrived, place = source(j)
        seq[0:EDGE, :] = jnp.where(arrived, e_arr[place], e_loc[j]).astype(F32)
        seq[EDGE:EDGE + FR, :] = normed.astype(F32)
        rows = pl.ds(pl.multiple_of(j * FR, FR), FR)
        for c in range(D // 128):
            lanes = slice(128 * c, 128 * c + 128)
            total = taps[0, :, lanes] * seq[0:FR, lanes]
            for t in range(1, KERNEL):
                total = total + taps[t, :, lanes] * seq[t:t + FR, lanes]
            mid[rows, lanes] = frames[j, :, lanes].astype(F32) + total
        second[rows, :] = layer_norm(mid[rows, :], gains[1:2, :]).astype(BF16)
        return carry

    def serve(rings, h, k, roles=(0, 1)):
        for role in roles:
            @pl.when(core == role)
            def _():
                rings[role].serve(h, k)

    def front_two(i):
        lax.fori_loop(2 * i, 2 * i + 2, front, 0)

    serve(ring_q, 0, 1)
    serve(ring_q, 1, 1)
    for r in range(4):
        book.arrive(None, lambda: copy_e(r), ("e", r))
    front_two(0)
    front_two(1)

    def compact(role):
        spread_o[role].arrive(0)
        for p in range(RING):
            tmp_o[12 * p:12 * p + 12, :] = p1o[p].astype(F32)
        for h in range(2):
            lanes = slice(PART * h, PART * h + PART)
            bufo[role, h, across[role]] = tmp_o[:, lanes].astype(BF16)
            ring_o[role].start(h)

    serve(ring_q, 0, 2)
    by_role(compact)
    front_two(2)
    serve(ring_q, 1, 2)
    front_two(3)
    serve(ring_q, 0, 3)
    front_two(4)
    serve(ring_q, 1, 3)
    front_two(5)
    serve(ring_o, 0, 1)
    serve(ring_o, 1, 1)
    serve(ring_q, 0, 4, (1,))
    serve(ring_q, 1, 4, (1,))

    def project(role, h):
        @pl.when(core == 1 - role)
        def _():
            ring_q[role].shared(1 - role, (h,))

        n = WIDTHS[role] // 2
        total = jnp.zeros((SLOTS * FR, n), F32)
        for g in range(4):
            part = bufq[role][h, 2 * g:2 * g + 2].astype(F32).reshape(384, n)
            total = total + jnp.dot(
                second[:, 384 * g:384 * g + 384], part.astype(BF16),
                preferred_element_type=F32,
            )
        for m in range(0, n, PART):
            to = STARTS[role] + 2 * m + PART * h
            proj[:, to:to + PART] = total[:, m:m + PART].astype(BF16)

    project(1, 0)
    project(1, 1)
    serve(ring_q, 0, 4, (0,))
    serve(ring_o, 0, 2)
    serve(ring_o, 1, 2)
    project(0, 0)
    serve(ring_q, 1, 4, (0,))
    serve(ring_o, 0, 3)
    serve(ring_o, 1, 3)
    project(0, 1)
    for r in range(4):
        book.arrive(None, lambda: copy_c(r), ("c", r))

    key_pos = lax.broadcasted_iota(jnp.int32, (HEADS * FR, CTX + FR), 1)
    frame = lax.rem(lax.broadcasted_iota(jnp.int32, (HEADS * FR, CTX + FR), 0), FR)

    def attend(group):
        rows = [slice(FR * j, FR * j + FR) for j in group]
        scores, values = [], []
        for j, at_rows in zip(group, rows):
            arrived, place = source(j)
            cached = jnp.where(arrived, c_arr[place], c_loc[j])
            keys = jnp.concatenate([cached[:, :HD], proj[at_rows, HD:2 * HD]], axis=0)
            values.append(
                jnp.concatenate([cached[:, HD:], proj[at_rows, 2 * HD:]], axis=0)
            )
            parts = []
            for n, ((low, high), (top, end)) in enumerate(zip(TILES, TILE_ROWS)):
                lanes = slice(256 * n, 256 * n + 256)
                q = jnp.concatenate([proj[at_rows, lanes]] * (high - low), axis=0)
                parts.append(lax.dot_general(
                    q * hmask[top:end, :], keys[:, lanes], (((1,), (1,)), ((), ())),
                    preferred_element_type=F32,
                ))
            s0, s1, s2 = parts
            scores.append(jnp.concatenate(
                [s0[:32], s0[32:] + s1[:16], s1[16:48], s1[48:] + s2[:16], s2[16:]], axis=0
            ) * HSIZE ** (-0.5))
        probs = []
        for j, score in zip(group, scores):
            allowed = ((key_pos < CTX) & (key_pos >= CTX - lengths[j])) | (
                (key_pos >= CTX) & (key_pos - CTX <= frame)
            )
            score = jnp.where(allowed, score, -1e30)
            weights = jnp.exp(score - jnp.max(score, axis=-1, keepdims=True))
            total = jnp.sum(weights, axis=-1, keepdims=True)
            probs.append((weights / total).astype(BF16))
        for at_rows, prob, value in zip(rows, probs, values):
            for n, ((low, high), (top, end)) in enumerate(zip(TILES, TILE_ROWS)):
                lanes = slice(256 * n, 256 * n + 256)
                wide = jnp.dot(
                    prob[FR * low:FR * high], value[:, lanes], preferred_element_type=F32
                ) * fmask[top:end, :]
                total = wide[0:FR]
                for hd in range(1, high - low):
                    total = total + wide[FR * hd:FR * hd + FR]
                ctx[at_rows, lanes] = total.astype(BF16)

    def hand(n):
        span = pl.ds(GROUP * n, GROUP)
        return remote(ostage.at[span], out.at[span], h_send, h_recv, n, next_sec)

    for n in range(SLOTS // GROUP):
        group = range(GROUP * n, GROUP * n + GROUP)
        attend(group)
        if n == 0:
            serve(ring_o, 0, 4)
            serve(ring_o, 1, 4)
            for role in range(2):
                @pl.when(core == 1 - role)
                def _():
                    ring_o[role].shared(1 - role)
        rows = slice(FR * GROUP * n, FR * GROUP * n + FR * GROUP)
        context = ctx[rows, :]
        turned = jnp.dot(context, order[...], preferred_element_type=F32).astype(BF16)
        for half in range(2):
            for part in range(2):
                at_lane = OH * half + PART * part
                lanes = slice(at_lane, at_lane + PART)
                weights = bufo[half, part].reshape(HD, PART)
                result = jnp.dot(
                    turned if half else context, weights, preferred_element_type=F32
                ) + mid[rows, lanes]
                for m, j in enumerate(group):
                    live = counts[0] > j
                    ostage[j, :, lanes] = jnp.where(
                        live, result[FR * m:FR * m + FR], 0.0
                    ).astype(BF16)
        book.start(None, lambda n=n: hand(n), ("h", n))

    by_role(book.close)
    book.close(None)
    for r in range(4):
        @pl.when(crossing[r])
        def _():
            book.close(("z", r))

        @pl.when(jnp.logical_not(crossing[r]))
        def _():
            book.close(("d", r))


def body(
    new_frames, conv_edges, kv_cache, norm_gains, conv_kernel,
    w_qkv, w_out, move_targets, lengths, counts,
):
    vmem = pl.BlockSpec(memory_space=pltpu.VMEM)
    smem = pl.BlockSpec(memory_space=pltpu.SMEM)
    any_ = pl.BlockSpec(memory_space=pl.ANY)
    dma = pltpu.SemaphoreType.DMA
    rows = SLOTS * FR
    out = pl.pallas_call(
        kernel,
        out_shape=jax.ShapeDtypeStruct((SLOTS, FR, D), BF16),
        in_specs=[any_, any_, any_, vmem, any_, any_, any_, smem, smem, smem],
        out_specs=any_,
        scratch_shapes=[
            pltpu.VMEM((SLOTS, FR, D), BF16),
            pltpu.VMEM((KERNEL, 1, D), F32),
            pltpu.VMEM((12, QW), BF16),
            pltpu.VMEM((6, D), BF16),
            pltpu.VMEM((SLOTS, EDGE, D), BF16),
            pltpu.VMEM((SLOTS, CTX, D), BF16),
            pltpu.VMEM((4, EDGE, D), BF16),
            pltpu.VMEM((4, CTX, D), BF16),
            pltpu.VMEM((4, EDGE, D), BF16),
            pltpu.VMEM((4, CTX, D), BF16),
            pltpu.VMEM((2, EDGE, D), BF16),
            pltpu.VMEM((2, CTX, D), BF16),
            pltpu.VMEM((12, WIDTHS[0]), BF16),
            pltpu.VMEM((12, WIDTHS[1]), BF16),
            pltpu.VMEM((6, OH), BF16),
            pltpu.VMEM((2, RING, RING, 24, WIDTHS[0] // 2), BF16),
            pltpu.VMEM((2, RING, RING, 24, WIDTHS[1] // 2), BF16),
            pltpu.VMEM((RING, 12, OH), BF16),
            pltpu.VMEM((2, 2, RING, 96, PART), BF16),
            pltpu.VMEM((24, WIDTHS[0] // 2), F32),
            pltpu.VMEM((96, OH), F32),
            pltpu.VMEM((48, D), F32),
            pltpu.VMEM((rows, D), F32),
            pltpu.VMEM((rows, D), BF16),
            pltpu.VMEM((rows, QW), BF16),
            pltpu.VMEM((rows, HD), BF16),
            pltpu.VMEM((160, 256), BF16),
            pltpu.VMEM((160, 256), F32),
            pltpu.VMEM((HD, HD), BF16),
            pltpu.VMEM((SLOTS, FR, D), BF16),
            dma((6,)), dma((2,)), dma((2,)), dma((8,)), dma((8,)),
            dma((16,)), dma((16,)), dma((8,)), dma((8,)),
            dma((16,)), dma((16,)), dma((16,)), dma((16,)),
            dma((18,)), dma((18,)), dma((18,)), dma((18,)),
            dma((4,)), dma((4,)), dma((4,)), dma((4,)),
        ],
        compiler_params=pltpu.CompilerParams(
            collective_id=0, has_side_effects=True, vmem_limit_bytes=56 * 2 ** 20
        ),
        cost_estimate=pl.CostEstimate(
            flops=2 * 10 ** 9, bytes_accessed=6 * 10 ** 6, transcendentals=10 ** 5
        ),
    )(
        new_frames[0], conv_edges[0], kv_cache[0], norm_gains[0], conv_kernel.transpose(1, 0, 2),
        w_qkv[0], w_out[0], move_targets, lengths, counts,
    )
    return out[None]


def solution(mesh):
    placed = (
        P("section", "sess", None, None),
        P("section", "sess", None, None),
        P("section", "sess", None, None),
        P("section", None, None),
        P("section", None, None),
        P("section", "sess", None),
        P("section", "sess", None),
        P("sess"),
        P("sess"),
        P("sess"),
    )
    return jax.shard_map(
        body,
        mesh=mesh,
        in_specs=placed,
        out_specs=P("section", "sess", None, None),
        check_vma=False,
    )
```

time: 227 us -> 90.6 us (0.40)
  waiting for transfers between devices: 99 us -> 0 us
  Pallas kernels: 0 us -> 87.8 us
  starting transfers between devices: 41.9 us -> 0 us
  other arithmetic: 25.8 us -> 0 us
  between operations: 21.9 us -> 0.66 us
  local copies, waits for them, and re-layouts: 20 us -> 1.92 us
  matrix products: 17.2 us -> 0 us
    pallas_call x0 -> x1, Pallas kernels: none -> 87.8 us  [body(): pl.pallas_call(kernel, out_shape=jax.ShapeDtypeStruct((SLOTS, FR, D), BF1...]
    all_gather x2 -> x0, waiting for transfers between devices: 84.3 us -> none  [the longest x1 57.2 us: section_compute(): lax.all_gather(out_rows, 'sess', axis=0, tiled=True)]
    ppermute x9 -> x0, starting transfers between devices: 41.8 us -> none  [passed_along(): return lax.ppermute(x, axis, [(i, (i + by) % size) for i in range(size)])]
    dot_general x4 -> x0, matrix products: 17.2 us -> none  [the longest x1 6.66 us: section_compute(): jnp.dot(columns, lax.all_gather(qkv_rows, 'sess', axis=0, tiled=True), pr...]
    ppermute x9 -> x0, waiting for transfers between devices: 14.7 us -> none  [passed_along(): return lax.ppermute(x, axis, [(i, (i + by) % size) for i in range(size)])]
    reshape x3 -> x0, local copies, waits for them, and re-layouts: 8.11 us -> none  [the longest x1 3.59 us: attend(): key_heads = keys.reshape(session_count, CTX + FR, HEADS, HSIZE)]
    reduce_sum x4 -> x0, other arithmetic: 7.84 us -> none  [the longest x2 7.28 us: layer_norm(): center = values - jnp.mean(values, axis=-1, keepdims=True)]
    scatter x8 -> x0, other arithmetic: 6.98 us -> none  [the longest x4 4.34 us: body(): moved_edges = moved_edges.at[slot_pick].set(arrived[0])]
  transfers between devices with their start and end apart: 11 -> 0, of which waited for: 3 -> 0; matrix products, arithmetic and copies ran while one was open for 24% -> 0% of each run, Pallas kernels for 0% -> 0%
where the time goes in v2:
time: 90.6 us; the launch traced here: 90.4 us
  Pallas kernels  87.8 us (97%)
  local copies, waits for them, and re-layouts  1.92 us (2%)
    pallas_call x1, Pallas kernels, body(): pl.pallas_call(kernel, out_shape=jax.ShapeDtypeStruct((SLOTS, FR, D), BF1...  87.8 us
    unnamed x1, local copies, waits for them, and re-layouts  1.92 us

profile of v2, /device:TPU:1, one launch (start us, length us, event | category | flops | bytes accessed | tf_op | source)
XLA Modules:
  0.0 90.4 jit_solution(11112985129082482383)
XLA Ops:
  0.7 87.8 %shard_map.100 = bf16[12,16,1536]{2,1,0:T(8,128)(2,1)} custom-call(bf16[12,16,1536]{2,1,0:T(8,128)(2,1)} %bitcast.11, bf16[12,30,1536]{2,1,0:T(8,128)(2,1)} %bitcast.10, bf16[12,64,1536]{2,1,0:T(8,128)(2,1)} %bitcast.9, f32[2,1536]{1,0:T(2,128)} %bitcast.15, f32[31,1,1536]{2,1,0:T(1,128)} %bitcast.12, bf16[12,2304]{1,0:T(8,128)(2,1)} %bitcast.13, ...), custom_call_target="tpu_custom_call" | custom-call | flops 2000000000 | bytes 6000000 | tf_op jit(solution)/shard_map/pallas_call | solution.py:594
  88.5 1.9 %copy.13 = bf16[1,12,16,1536]{3,2,1,0:T(8,128)(2,1)} copy(bf16[1,12,16,1536]{3,2,1,0:T(8,128)(2,1)} %bitcast.8) | data formatting | bytes 1179648

commit v3 on v2

--- a/solution.py
+++ b/solution.py
@@ -398,8 +398,6 @@
 
     by_role(start_q)
     pass_along(0)
-    leave(1)
-    pass_along(1)
 
     for i in range(HD // 128):
         shape = (HD, 128)
@@ -435,11 +433,10 @@
 
     serve(ring_q, 0, 1)
     serve(ring_q, 1, 1)
+    leave(1)
+    pass_along(1)
     for r in range(4):
         book.arrive(None, lambda: copy_e(r), ("e", r))
-    front_two(0)
-    front_two(1)
-
     def compact(role):
         spread_o[role].arrive(0)
         for p in range(RING):
@@ -449,8 +446,11 @@
             bufo[role, h, across[role]] = tmp_o[:, lanes].astype(BF16)
             ring_o[role].start(h)
 
+    by_role(compact)
+    front_two(0)
+    front_two(1)
+
     serve(ring_q, 0, 2)
-    by_role(compact)
     front_two(2)
     serve(ring_q, 1, 2)
     front_two(3)

time: 90.6 us -> 88.5 us (0.977)
  Pallas kernels: 87.8 us -> 85.7 us
    pallas_call x1, Pallas kernels: 87.8 us -> 85.7 us  [body(): pl.pallas_call(kernel, out_shape=jax.ShapeDtypeStruct((SLOTS, FR, D), BF1...]
where the time goes in v3:
time: 88.5 us; the launch traced here: 88.3 us
  Pallas kernels  85.7 us (97%)
  local copies, waits for them, and re-layouts  1.92 us (2%)
    pallas_call x1, Pallas kernels, body(): pl.pallas_call(kernel, out_shape=jax.ShapeDtypeStruct((SLOTS, FR, D), BF1...  85.7 us
    unnamed x1, local copies, waits for them, and re-layouts  1.92 us

profile of v3, /device:TPU:1, one launch (start us, length us, event | category | flops | bytes accessed | tf_op | source)
XLA Modules:
  0.0 88.3 jit_solution(663301015043712081)
XLA Ops:
  0.7 85.7 %shard_map.100 = bf16[12,16,1536]{2,1,0:T(8,128)(2,1)} custom-call(bf16[12,16,1536]{2,1,0:T(8,128)(2,1)} %bitcast.11, bf16[12,30,1536]{2,1,0:T(8,128)(2,1)} %bitcast.10, bf16[12,64,1536]{2,1,0:T(8,128)(2,1)} %bitcast.9, f32[2,1536]{1,0:T(2,128)} %bitcast.15, f32[31,1,1536]{2,1,0:T(1,128)} %bitcast.12, bf16[12,2304]{1,0:T(8,128)(2,1)} %bitcast.13, ...), custom_call_target="tpu_custom_call" | custom-call | flops 2000000000 | bytes 6000000 | tf_op jit(solution)/shard_map/pallas_call | solution.py:594
  86.3 1.9 %copy.13 = bf16[1,12,16,1536]{3,2,1,0:T(8,128)(2,1)} copy(bf16[1,12,16,1536]{3,2,1,0:T(8,128)(2,1)} %bitcast.8) | data formatting | bytes 1179648

commit v4 on v3

--- a/solution.py
+++ b/solution.py
@@ -455,11 +455,13 @@
     serve(ring_q, 1, 2)
     front_two(3)
     serve(ring_q, 0, 3)
+    serve(ring_o, 0, 1)
+    serve(ring_o, 1, 1)
     front_two(4)
     serve(ring_q, 1, 3)
+    serve(ring_o, 0, 2)
+    serve(ring_o, 1, 2)
     front_two(5)
-    serve(ring_o, 0, 1)
-    serve(ring_o, 1, 1)
     serve(ring_q, 0, 4, (1,))
     serve(ring_q, 1, 4, (1,))
 
@@ -483,12 +485,10 @@
     project(1, 0)
     project(1, 1)
     serve(ring_q, 0, 4, (0,))
-    serve(ring_o, 0, 2)
-    serve(ring_o, 1, 2)
+    serve(ring_o, 0, 3)
+    serve(ring_o, 1, 3)
     project(0, 0)
     serve(ring_q, 1, 4, (0,))
-    serve(ring_o, 0, 3)
-    serve(ring_o, 1, 3)
     project(0, 1)
     for r in range(4):
         book.arrive(None, lambda: copy_c(r), ("c", r))

time: 88.5 us -> 86.1 us (0.973)
  Pallas kernels: 85.7 us -> 83.3 us
    pallas_call x1, Pallas kernels: 85.7 us -> 83.3 us  [body(): pl.pallas_call(kernel, out_shape=jax.ShapeDtypeStruct((SLOTS, FR, D), BF1...]
where the time goes in v4:
time: 86.1 us; the launch traced here: 85.9 us
  Pallas kernels  83.3 us (97%)
  local copies, waits for them, and re-layouts  1.92 us (2%)
    pallas_call x1, Pallas kernels, body(): pl.pallas_call(kernel, out_shape=jax.ShapeDtypeStruct((SLOTS, FR, D), BF1...  83.3 us
    unnamed x1, local copies, waits for them, and re-layouts  1.92 us

profile of v4, /device:TPU:1, one launch (start us, length us, event | category | flops | bytes accessed | tf_op | source)
XLA Modules:
  0.0 85.9 jit_solution(17056778352200744251)
XLA Ops:
  0.7 83.3 %shard_map.100 = bf16[12,16,1536]{2,1,0:T(8,128)(2,1)} custom-call(bf16[12,16,1536]{2,1,0:T(8,128)(2,1)} %bitcast.11, bf16[12,30,1536]{2,1,0:T(8,128)(2,1)} %bitcast.10, bf16[12,64,1536]{2,1,0:T(8,128)(2,1)} %bitcast.9, f32[2,1536]{1,0:T(2,128)} %bitcast.15, f32[31,1,1536]{2,1,0:T(1,128)} %bitcast.12, bf16[12,2304]{1,0:T(8,128)(2,1)} %bitcast.13, ...), custom_call_target="tpu_custom_call" | custom-call | flops 2000000000 | bytes 6000000 | tf_op jit(solution)/shard_map/pallas_call | solution.py:594
  83.9 1.9 %copy.13 = bf16[1,12,16,1536]{3,2,1,0:T(8,128)(2,1)} copy(bf16[1,12,16,1536]{3,2,1,0:T(8,128)(2,1)} %bitcast.8) | data formatting | bytes 1179648
